TPU v7x, 32 devices: a whole 2x2x4 slice. The times are simulated.
32 devices in a mesh: groups: 2 (over y), cell: 8 (over z, x), dp: 2 (over core).
Axes of the slice: x: 2, y: 2, z: 4, core: 2. Of those that a mesh axis runs over, the one named last changes fastest.
Arguments:
- sensitivity: bfloat16 [8192, 8192], P(('groups', 'dp'), 'cell'), parts along dimension 0, may hold values from -127 to 127
- block_scale: float32 [64, 64], P(('groups', 'dp'), 'cell'), parts along dimension 0, may hold values from 1.5134991e-05 to 0.00136214919
- depth_weight: float32 [16384], P(('groups', 'cell')), parts along dimension 0, may hold values from 0.05 to 1.5
- model: float32 [128, 8192], P('groups', 'cell'), parts along dimension 0, may hold values from -6 to 6
- residual: float32 [128, 4096], P('groups', 'dp'), parts along dimension 0, may hold values from -6 to 6
- direction: float32 [128, 8192], P('groups', 'cell'), parts along dimension 0, may hold values from -3 to 3
- gamma: float32 [128], P('groups'), parts along dimension 0, may hold values from 8192 to 32768
Outputs:
- model_new: float32 [128, 8192], P('groups', 'cell'), parts along dimension 0
- residual_new: float32 [128, 4096], P('groups', 'dp'), parts along dimension 0
- direction_new: float32 [128, 8192], P('groups', 'cell'), parts along dimension 0
- gamma_new: float32 [128], P('groups'), parts along dimension 0
There are 2 independent parts, one for each index of `groups`. A program takes and returns all parts, laid end to end along the dimension named above; each array names one. Nothing has to cross between parts.
All inputs are finite; a program needn't handle non-finite values.
Results may differ from a plain program's by a relative error of at most 0.0025.
Values sent between devices are 32-bit elements; how exact they have to be, the bound alone decides.
A program may use at most 64 MiB of HBM per device.

v0:
```python
import jax
import jax.numpy as jnp
from jax import lax
from jax.sharding import PartitionSpec as P

EPSILON = 1e-06


def local(sensitivity, block_scale, depth_weight, model, residual, direction, gamma):
    row_count, col_count = sensitivity.shape
    set_count = direction.shape[0]
    row_blocks = row_count // 128
    col_blocks = col_count // 128
    blocks = sensitivity.reshape(row_blocks, 128, col_blocks, 128)
    scaled = (direction / depth_weight[None, :]).astype(jnp.bfloat16)
    tile_sums = jnp.einsum(
        "aibj,kbj->kabi",
        blocks,
        scaled.reshape(set_count, col_blocks, 128),
        preferred_element_type=jnp.float32,
    )
    partial_value = jnp.sum(tile_sums * block_scale[None, :, :, None], axis=2).reshape(
        set_count, row_count
    )
    predicted = lax.psum(partial_value, "cell")
    curvature = lax.psum(jnp.sum(predicted * predicted, axis=1), "dp")
    step_len = gamma / (curvature + EPSILON)
    residual_new = residual - step_len[:, None] * predicted
    model_new = model + step_len[:, None] * direction
    weighted = residual_new.astype(jnp.bfloat16)
    back_tiles = jnp.einsum(
        "aibj,kai->kabj",
        blocks,
        weighted.reshape(set_count, row_blocks, 128),
        preferred_element_type=jnp.float32,
    )
    partial_grad = jnp.sum(back_tiles * block_scale[None, :, :, None], axis=1).reshape(
        set_count, col_count
    )
    gradient = lax.psum(partial_grad, "dp") / depth_weight[None, :]
    gamma_new = lax.psum(jnp.sum(gradient * gradient, axis=1), "cell")
    direction_new = gradient + (gamma_new / gamma)[:, None] * direction
    return (model_new, residual_new, direction_new, gamma_new)


def solution(mesh):
    in_specs = (
        P(("groups", "dp"), "cell"),
        P(("groups", "dp"), "cell"),
        P(("groups", "cell")),
        P("groups", "cell"),
        P("groups", "dp"),
        P("groups", "cell"),
        P("groups"),
    )
    out_specs = (P("groups", "cell"), P("groups", "dp"), P("groups", "cell"), P("groups"))
    return jax.shard_map(local, mesh=mesh, in_specs=in_specs, out_specs=out_specs, check_vma=False)
```

profile of v0, /device:TPU:0, one launch (start us, length us, event | category | flops | bytes accessed | tf_op | source)
XLA Modules:
  0.0 147.3 jit_solution(13891848506391469080)
XLA Ops:
  7.2 0.0 all-reduce.3.cloned.1.call-start
  7.2 0.0 copy-start.1
  7.2 0.0 copy-start.4
  7.2 3.3 %copy.37 = bf16[256,8,8,128]{3,2,1,0:T(8,128)(2,1)S(1)} copy(bf16[256,8,8,128]{3,1,2,0:T(8,128)(2,1)} %bitcast.27) | data formatting | bytes 8388608
  10.7 0.0 copy-start.6
  10.7 0.0 copy-start.2
  10.7 1.8 %fusion = f32[64,16,128]{2,0,1:T(8,128)S(1)} fusion(f32[16,8]{0,1:T(8,128)S(1)} %copy-done.5, bf16[16,128,8,128]{3,2,1,0:T(8,128)(2,1)S(1)} %bitcast.28, bf16[64,8,128,1]{2,1,0,3:T(8,128)(2,1)S(1)} %bitcast.31), kind=kOutput, calls=%fused_computation.1 | convolution fusion | flops 270401536 | bytes 4850176 | tf_op jit(solution)/shard_map/aibj,kbj->kabi/dot_general | solution.py:16
  12.5 0.0 copy-done
  12.5 0.8 copy_bitcast_fusion
  13.3 0.0 all-reduce.3.cloned.1.call-update
  13.4 0.0 all-reduce.5.cloned.1.call-start
  13.4 0.1 copy.26
  13.5 75.1 %all-reduce.3.cloned.1.call-done = f32[64,2048]{1,0:T(8,128)} async-done(((f32[64,2048]{1,0:T(8,128)}), f32[64,2048]{1,0:T(8,128)}) %all-reduce.3.cloned.1.call-update) | async-done | bytes 524304 | tf_op jit(solution)/shard_map/psum | solution.py:25
  88.6 1.2 multiply_reduce_fusion.1
  89.8 2.5 %psum.29 = f32[64]{0:T(128)S(1)} all-reduce(f32[64]{0:T(128)S(1)} %multiply_reduce_fusion.1), channel_id=1, replica_groups=mesh['groups'=2,'cell'=8,'dp'=2] {'dp'}, use_global_device_ids=true, to_apply=%region_3.0 | all-reduce | flops 64 | bytes 512 | tf_op jit(solution)/shard_map/psum | solution.py:26
  92.2 0.0 copy-done.6
  92.3 2.0 %convert_bitcast_fusion = (bf16[8,8,16,128]{3,1,2,0:T(8,128)(2,1)S(1)}, f32[64,2048]{1,0:T(8,128)}) fusion(f32[64,2048]{1,0:T(8,128)S(1)} %copy-done.2, f32[64,2048]{1,0:T(8,128)} %all-reduce.3.cloned.1.call-done, f32[64]{0:T(128)S(1)} %add_divide_fusion), kind=kLoop, calls=%fused_computation.14 | loop fusion | flops 393216 | bytes 1835264
  94.3 3.1 %multiply_reduce_fusion = f32[64,8,128]{2,0,1:T(8,128)S(1)} fusion(bf16[16,128,8,128]{3,2,1,0:T(8,128)(2,1)} %bitcast.29, f32[16,8]{1,0:T(8,128)S(1)} %copy.26, bf16[64,16,128,1]{2,1,0,3:T(8,128)(2,1)S(1)} %bitcast.30), kind=kOutput, calls=%fused_computation.6 | convolution fusion | flops 270467072 | bytes 4719104 | tf_op jit(solution)/shard_map/aibj,kai->kabj/dot_general | solution.py:31
  97.4 0.7 copy_bitcast_fusion.1
  98.1 0.0 all-reduce.5.cloned.1.call-update
  98.2 17.7 %all-reduce.5.cloned.1.call-done = f32[64,1024]{1,0:T(8,128)} async-done(((f32[64,1024]{1,0:T(8,128)}), f32[64,1024]{1,0:T(8,128)}) %all-reduce.5.cloned.1.call-update) | async-done | bytes 262160 | tf_op jit(solution)/shard_map/psum | solution.py:40
  115.9 1.1 multiply_reduce_fusion.2
  117.0 21.6 %psum.31 = f32[64]{0:T(128)S(1)} all-reduce(f32[64]{0:T(128)S(1)} %multiply_reduce_fusion.2), channel_id=1, replica_groups=mesh['groups'=2,'cell'=8,'dp'=2] {'cell'}, use_global_device_ids=true, to_apply=%region_7.0 | all-reduce | flops 64 | bytes 512 | tf_op jit(solution)/shard_map/psum | solution.py:41
  138.6 1.9 %multiply_add_fusion = (f32[64,1024]{1,0:T(8,128)}, f32[64,1024]{1,0:T(8,128)}) fusion(f32[64,1024]{1,0:T(8,128)S(1)} %copy-done.1, f32[64]{0:T(128)S(1)} %div.24, f32[64,1024]{1,0:T(8,128)} %all-reduce.5.cloned.1.call-done, f32[1024]{0:T(1024)S(1)} %copy-done.4, f32[64,1024]{1,0:T(8,128)S(1)} %copy-done.3, f32[64]{0:T(128)S(1)} %add_divide_fusion), kind=kLoop, calls=%fused_computation.12 | loop fusion | flops 327680 | bytes 1315328 | tf_op jit(solution)/shard_map/add | solution.py:42
  (15 shorter events, 0.1 us)
Async XLA Ops:
  7.2 81.4 %all-reduce.3.cloned.1.call-start = ((), (), s32[]{:S(2)}) async-start(), calls=%async_computation | async-start | bytes 1048576 | tf_op jit(solution)/shard_map/psum | solution.py:25
  7.2 3.4 %copy-start.1 = (f32[64,1024]{1,0:T(8,128)S(1)}, f32[64,1024]{1,0:T(8,128)}, u32[]{:S(2)}) copy-start(f32[64,1024]{1,0:T(8,128)} %param.12) | copy-start | bytes 786436
  7.2 3.4 %copy-start.4 = (f32[1024]{0:T(1024)S(1)}, f32[1024]{0:T(1024)}, u32[]{:S(2)}) copy-start(f32[1024]{0:T(1024)} %param.9) | copy-start | bytes 12292
  7.2 3.4 %copy-start.5 = (f32[16,8]{0,1:T(8,128)S(1)}, f32[16,8]{0,1:T(8,128)}, u32[]{:S(2)}) copy-start(f32[16,8]{0,1:T(8,128)} %param.8) | copy-start | bytes 1540
  10.6 1.9 %copy-start = (bf16[256,8,8,128]{3,2,1,0:T(8,128)(2,1)}, bf16[256,8,8,128]{3,2,1,0:T(8,128)(2,1)S(1)}, u32[]{:S(2)}) copy-start(bf16[256,8,8,128]{3,2,1,0:T(8,128)(2,1)S(1)} %copy.37) | copy-start | bytes 12582916
  10.7 81.6 %copy-start.6 = (f32[64]{0:T(128)S(1)}, f32[64]{0:T(128)}, u32[]{:S(2)}) copy-start(f32[64]{0:T(128)} %param.13) | copy-start | bytes 772
  10.7 81.6 %copy-start.2 = (f32[64,2048]{1,0:T(8,128)S(1)}, f32[64,2048]{1,0:T(8,128)}, u32[]{:S(2)}) copy-start(f32[64,2048]{1,0:T(8,128)} %param.11) | copy-start | bytes 1572868
  13.4 102.5 %all-reduce.5.cloned.1.call-start = ((), (), s32[]{:S(2)}) async-start(), calls=%async_computation.1 | async-start | bytes 524288 | tf_op jit(solution)/shard_map/psum | solution.py:40
  94.2 44.4 %copy-start.3 = (f32[64,1024]{1,0:T(8,128)S(1)}, f32[64,1024]{1,0:T(8,128)}, u32[]{:S(2)}) copy-start(f32[64,1024]{1,0:T(8,128)} %param.10) | copy-start | bytes 786436
  138.6 1.9 %copy-start.7 = (f32[64]{0:T(128)}, f32[64]{0:T(128)S(1)}, u32[]{:S(2)}) copy-start(f32[64]{0:T(128)S(1)} %psum.31) | copy-start | bytes 772
Sparse Core Ops, SparseCore 0:
  13.5 75.0 all-reduce.2
  98.3 17.5 all-reduce.4
where the time goes:
time: 148 us; the launch traced here: 147 us
  waiting for transfers between devices  92.8 us (63%)
  blocking collectives  24.1 us (16%)
  between operations  14.2 us (10%)
  other arithmetic  6.12 us (4%)
  local copies, waits for them, and re-layouts  5.04 us (3%)
  matrix products  4.93 us (3%)
    psum x1, waiting for transfers between devices, local(): predicted = lax.psum(partial_value, 'cell')  75.1 us
    psum x1, blocking collectives, local(): gamma_new = lax.psum(jnp.sum(gradient * gradient, axis=1), 'cell')  21.6 us
    psum x1, waiting for transfers between devices, local(): gradient = lax.psum(partial_grad, 'dp') / depth_weight[None, :]  17.7 us
    unnamed x20, local copies, waits for them, and re-layouts  3.49 us
    dot_general x1, matrix products, local(): jnp.einsum('aibj,kai->kabj', blocks, weighted.reshape(set_count, row_bloc...  3.14 us
  transfers between devices with their start and end apart: 2, of which 2 were waited for; matrix products, arithmetic and copies ran while one was open for 0% of the time, Pallas kernels for 0%

commit v1 on v0

v1 whole, which is shorter than its diff:
```python
import functools

import jax
import jax.numpy as jnp
from jax import lax
from jax.experimental import pallas as pl
from jax.experimental.pallas import tpu as pltpu
from jax.sharding import PartitionSpec as P

EPSILON = 1e-06
BLOCK = 128
MESH = pl.DeviceIdType.MESH


def to_row(column, first):
    shape = (column.shape[0], 128)
    place = lax.broadcasted_iota(jnp.int32, shape, 0) + first
    lane = lax.broadcasted_iota(jnp.int32, shape, 1)
    return jnp.sum(jnp.where(place == lane, column, 0.0), axis=0, keepdims=True)


def to_column(row, count):
    shape = (count, 128)
    place = lax.broadcasted_iota(jnp.int32, shape, 0)
    lane = lax.broadcasted_iota(jnp.int32, shape, 1)
    return jnp.sum(jnp.where(place == lane, row, 0.0), axis=1, keepdims=True)


def kernel(
    n, nr, ns,
    sens_hbm, scale, depth, model_hbm, resid_hbm, direc_hbm, gamma,
    model_out, resid_out, direc_out, gamma_out,
    sens, model, resid, direc, scaled, part, recv, pred, curv, grad, other, gams,
    sens_sem, load_sem, out_sem,
    rs_send, rs_recv, ag_send, ag_recv, cv_send, cv_recv, dp_send, dp_recv, gm_send, gm_recv,
):
    sets, cells = direc.shape
    cs, cr = recv.shape[1:]
    row_blocks = cr // BLOCK
    col_blocks = cells // BLOCK
    pieces = grad.shape[0]
    width = grad.shape[2]
    total = 2 * n
    me = lax.axis_index("cell")
    core = lax.axis_index("dp")
    rank = me * 2 + core
    my_q = me // ns
    my_g = me % ns

    def sens_copy(t):
        q = lax.rem(my_q + 1 + t, nr)
        return pltpu.make_async_copy(
            sens_hbm.at[pl.ds(pl.multiple_of(q * cr, cr), cr), :], sens.at[t], sens_sem.at[t]
        )

    direc_load = pltpu.make_async_copy(direc_hbm, direc, load_sem.at[0])
    direc_load.start()
    for t in range(nr):
        sens_copy(t).start()
    resid_load = pltpu.make_async_copy(resid_hbm, resid, load_sem.at[1])
    resid_load.start()
    model_load = pltpu.make_async_copy(model_hbm, model, load_sem.at[2])
    model_load.start()

    barrier = pltpu.get_barrier_semaphore()

    def greet(t, _):
        peer = lax.rem(rank + t, total)
        pl.semaphore_signal(
            barrier, inc=1, device_id={"cell": peer // 2, "dp": lax.rem(peer, 2)}, device_id_type=MESH
        )
        return 0

    lax.fori_loop(1, total, greet, 0)

    inverse = 1.0 / depth[...].reshape(1, cells)
    gamma_row = jnp.concatenate(
        [gamma[...].reshape(1, sets), jnp.ones((1, 128 - sets), jnp.float32)], axis=1
    )
    direc_load.wait()
    scaled[...] = (direc[...] * inverse).astype(jnp.bfloat16)
    pl.semaphore_wait(barrier, total - 1)

    def rs_copy(q, g):
        j = q * ns + g
        return pltpu.make_async_remote_copy(
            src_ref=part.at[q, pl.ds(pl.multiple_of(g * cs, cs), cs), :],
            dst_ref=recv.at[me],
            send_sem=rs_send.at[j],
            recv_sem=rs_recv.at[me],
            device_id={"cell": j},
            device_id_type=MESH,
        )

    def forward(t, _):
        q = lax.rem(my_q + 1 + t, nr)
        sens_copy(t).wait()
        accs = [None] * row_blocks
        for b in range(col_blocks):
            tile = lax.dot_general(
                scaled[:, b * BLOCK:(b + 1) * BLOCK],
                sens[t, :, b * BLOCK:(b + 1) * BLOCK],
                (((1,), (1,)), ((), ())),
                preferred_element_type=jnp.float32,
            )
            for a in range(row_blocks):
                term = tile[:, a * BLOCK:(a + 1) * BLOCK] * scale[q * row_blocks + a, b]
                accs[a] = term if accs[a] is None else accs[a] + term
        for a in range(row_blocks):
            part[q, :, a * BLOCK:(a + 1) * BLOCK] = accs[a]

        def send(g, _):
            @pl.when(q * ns + g != me)
            def _():
                rs_copy(q, g).start()
            return 0

        lax.fori_loop(0, ns, send, 0)
        return 0

    lax.fori_loop(0, nr, forward, 0)

    mine = pl.ds(pl.multiple_of(my_g * cs, cs), cs)

    def rs_arrival(src):
        return pltpu.make_async_remote_copy(
            src_ref=recv.at[src], dst_ref=recv.at[src], send_sem=rs_send.at[src],
            recv_sem=rs_recv.at[src], device_id={"cell": src}, device_id_type=MESH,
        )

    pred[my_q, mine, :] = part[my_q, mine, :]

    def reduce(t, _):
        src = lax.rem(me + t, n)
        rs_arrival(src).wait_recv()
        pred[my_q, mine, :] += recv[src]
        return 0

    lax.fori_loop(1, n, reduce, 0)

    value = pred[my_q, mine, :]
    curv[rank] = to_row(jnp.sum(value * value, axis=1, keepdims=True), my_g * cs)

    def cv_copy(slot, peer):
        return pltpu.make_async_remote_copy(
            src_ref=curv.at[slot], dst_ref=curv.at[slot], send_sem=cv_send.at[peer],
            recv_sem=cv_recv.at[slot],
            device_id={"cell": peer // 2, "dp": lax.rem(peer, 2)}, device_id_type=MESH,
        )

    def cv_start(t, _):
        cv_copy(rank, lax.rem(rank + t, total)).start()
        return 0

    lax.fori_loop(1, total, cv_start, 0)

    def ag_copy(q, g, peer):
        ref = pred.at[q, pl.ds(pl.multiple_of(g * cs, cs), cs), :]
        return pltpu.make_async_remote_copy(
            src_ref=ref, dst_ref=ref, send_sem=ag_send.at[peer],
            recv_sem=ag_recv.at[q * ns + g], device_id={"cell": peer}, device_id_type=MESH,
        )

    def ag_start(t, _):
        ag_copy(my_q, my_g, lax.rem(me + t, n)).start()
        return 0

    lax.fori_loop(1, n, ag_start, 0)

    def cv_wait(t, _):
        peer = lax.rem(rank + t, total)
        cv_copy(peer, peer).wait_recv()
        return 0

    lax.fori_loop(1, total, cv_wait, 0)
    curvature = lax.fori_loop(
        0, total, lambda i, acc: acc + curv[i], jnp.zeros((1, 128), jnp.float32)
    )
    step = to_column(gamma_row / (curvature + EPSILON), sets)

    model_load.wait()
    model[...] = model[...] + step * direc[...]
    model_store = pltpu.make_async_copy(model, model_out, out_sem.at[0])
    model_store.start()
    resid_load.wait()
    grad[...] = jnp.zeros(grad.shape, jnp.float32)

    def backward(u, _):
        t = nr - 1 - u
        q = lax.rem(my_q + 1 + t, nr)

        def arrive(g, _):
            @pl.when(q * ns + g != me)
            def _():
                ag_copy(q, g, q * ns + g).wait_recv()
            return 0

        lax.fori_loop(0, ns, arrive, 0)
        where = pl.ds(pl.multiple_of(q * cr, cr), cr)
        fresh = resid[:, where] - step * pred[q]
        resid[:, where] = fresh
        weighted = fresh.astype(jnp.bfloat16)
        for p in range(pieces):
            acc = grad[p]
            for a in range(row_blocks):
                tile = jnp.dot(
                    weighted[:, a * BLOCK:(a + 1) * BLOCK],
                    sens[t, a * BLOCK:(a + 1) * BLOCK, p * width:(p + 1) * width],
                    preferred_element_type=jnp.float32,
                )
                acc = acc + jnp.concatenate(
                    [
                        tile[:, b * BLOCK:(b + 1) * BLOCK]
                        * scale[q * row_blocks + a, p * (width // BLOCK) + b]
                        for b in range(width // BLOCK)
                    ],
                    axis=1,
                )
            grad[p] = acc
        return 0

    lax.fori_loop(0, nr, backward, 0)

    def dp_copy(p):
        return pltpu.make_async_remote_copy(
            src_ref=grad.at[p], dst_ref=other.at[p], send_sem=dp_send.at[p],
            recv_sem=dp_recv.at[p], device_id={"dp": 1 - core}, device_id_type=MESH,
        )

    for p in range(pieces):
        dp_copy(p).start()
    resid_store = pltpu.make_async_copy(resid, resid_out, out_sem.at[1])
    resid_store.start()

    square = jnp.zeros((sets, 1), jnp.float32)
    for p in range(pieces):
        dp_copy(p).wait()
        full = (grad[p] + other[p]) * inverse[:, p * width:(p + 1) * width]
        grad[p] = full
        square = square + jnp.sum(full * full, axis=1, keepdims=True)
    gams[me] = to_row(square, 0)

    def gm_copy(slot, peer):
        return pltpu.make_async_remote_copy(
            src_ref=gams.at[slot], dst_ref=gams.at[slot], send_sem=gm_send.at[peer],
            recv_sem=gm_recv.at[slot], device_id={"cell": peer}, device_id_type=MESH,
        )

    def gm_start(t, _):
        gm_copy(me, lax.rem(me + t, n)).start()
        return 0

    def gm_wait(t, _):
        peer = lax.rem(me + t, n)
        gm_copy(peer, peer).wait_recv()
        return 0

    lax.fori_loop(1, n, gm_start, 0)
    lax.fori_loop(1, n, gm_wait, 0)
    gamma_new = lax.fori_loop(
        0, n, lambda i, acc: acc + gams[i], jnp.zeros((1, 128), jnp.float32)
    )
    gamma_out[...] = gamma_new[:, :sets].reshape(sets)
    ratio = to_column(gamma_new / gamma_row, sets)
    for p in range(pieces):
        span = slice(p * width, (p + 1) * width)
        direc[:, span] = grad[p] + ratio * direc[:, span]
    direc_store = pltpu.make_async_copy(direc, direc_out, out_sem.at[2])
    direc_store.start()

    def drain(t, _):
        peer = lax.rem(me + t, n)
        rs_arrival(peer).wait_send()
        ag_copy(my_q, my_g, peer).wait_send()
        gm_copy(me, peer).wait_send()
        return 0

    def cv_drain(t, _):
        cv_copy(rank, lax.rem(rank + t, total)).wait_send()
        return 0

    lax.fori_loop(1, n, drain, 0)
    lax.fori_loop(1, total, cv_drain, 0)
    model_store.wait()
    resid_store.wait()
    direc_store.wait()


def local(n, sensitivity, block_scale, depth_weight, model, residual, direction, gamma):
    rows, cells = sensitivity.shape
    sets = direction.shape[0]
    nr = min(n, rows // BLOCK)
    ns = n // nr
    cr, cs = rows // nr, sets // ns
    pieces = 4
    f32 = jnp.float32
    any_space = pl.BlockSpec(memory_space=pl.ANY)
    vmem = pl.BlockSpec(memory_space=pltpu.VMEM)
    smem = pl.BlockSpec(memory_space=pltpu.SMEM)
    dma = pltpu.SemaphoreType.DMA
    return pl.pallas_call(
        functools.partial(kernel, n, nr, ns),
        out_shape=(
            jax.ShapeDtypeStruct(model.shape, f32),
            jax.ShapeDtypeStruct(residual.shape, f32),
            jax.ShapeDtypeStruct(direction.shape, f32),
            jax.ShapeDtypeStruct(gamma.shape, f32),
        ),
        in_specs=[any_space, smem, vmem, any_space, any_space, any_space, vmem],
        out_specs=(any_space, any_space, any_space, vmem),
        scratch_shapes=[
            pltpu.VMEM((nr, cr, cells), jnp.bfloat16),
            pltpu.VMEM((sets, cells), f32),
            pltpu.VMEM((sets, rows), f32),
            pltpu.VMEM((sets, cells), f32),
            pltpu.VMEM((sets, cells), jnp.bfloat16),
            pltpu.VMEM((nr, sets, cr), f32),
            pltpu.VMEM((n, cs, cr), f32),
            pltpu.VMEM((nr, sets, cr), f32),
            pltpu.VMEM((2 * n, 1, 128), f32),
            pltpu.VMEM((pieces, sets, cells // pieces), f32),
            pltpu.VMEM((pieces, sets, cells // pieces), f32),
            pltpu.VMEM((n, 1, 128), f32),
            dma((nr,)), dma((3,)), dma((3,)),
            dma((n,)), dma((n,)), dma((n,)), dma((n,)),
            dma((2 * n,)), dma((2 * n,)), dma((pieces,)), dma((pieces,)),
            dma((n,)), dma((n,)),
        ],
        compiler_params=pltpu.CompilerParams(
            collective_id=0, has_side_effects=True, vmem_limit_bytes=32 * 1024 * 1024
        ),
        cost_estimate=pl.CostEstimate(
            flops=4 * rows * cells * sets, bytes_accessed=2 * rows * cells, transcendentals=0
        ),
        name="cgls_iteration",
    )(sensitivity, block_scale, depth_weight, model, residual, direction, gamma)


def solution(mesh):
    in_specs = (
        P(("groups", "dp"), "cell"),
        P(("groups", "dp"), "cell"),
        P(("groups", "cell")),
        P("groups", "cell"),
        P("groups", "dp"),
        P("groups", "cell"),
        P("groups"),
    )
    out_specs = (P("groups", "cell"), P("groups", "dp"), P("groups", "cell"), P("groups"))
    return jax.shard_map(
        functools.partial(local, mesh.shape["cell"]),
        mesh=mesh, in_specs=in_specs, out_specs=out_specs, check_vma=False,
    )
```

time: 148 us -> 53.2 us (0.36)
  waiting for transfers between devices: 92.8 us -> 0 us
  Pallas kernels: 0 us -> 42.3 us
  blocking collectives: 24.1 us -> 0 us
  between operations: 14.2 us -> 0.65 us
  other arithmetic: 6.12 us -> 0 us
  matrix products: 4.93 us -> 0 us
  local copies, waits for them, and re-layouts: 5.04 us -> 9.94 us
    psum x2 -> x0, waiting for transfers between devices: 92.8 us -> none  [the longest x1 75.1 us: local(): predicted = lax.psum(partial_value, 'cell')]
    pallas_call x0 -> x1, Pallas kernels: none -> 42.3 us  [local(): pl.pallas_call(functools.partial(kernel, n, nr, ns), out_shape=(jax.Shape...]
    psum x2 -> x0, blocking collectives: 24.1 us -> none  [the longest x1 21.6 us: local(): gamma_new = lax.psum(jnp.sum(gradient * gradient, axis=1), 'cell')]
    unnamed x20 -> x17, local copies, waits for them, and re-layouts: 3.49 us -> 9.94 us
    dot_general x2 -> x0, matrix products: 4.93 us -> none  [the longest x1 3.14 us: local(): jnp.einsum('aibj,kai->kabj', blocks, weighted.reshape(set_count, row_bloc...]
    reduce_sum x2 -> x0, other arithmetic: 2.26 us -> none  [the longest x1 1.18 us: local(): curvature = lax.psum(jnp.sum(predicted * predicted, axis=1), 'dp')]
    unnamed x2 -> x0, other arithmetic: 2 us -> none
    add x1 -> x0, other arithmetic: 1.85 us -> none  [local(): direction_new = gradient + (gamma_new / gamma)[:, None] * direction]
  transfers between devices with their start and end apart: 2 -> 0, of which waited for: 2 -> 0; matrix products, arithmetic and copies ran while one was open for 0% -> 0% of each run, Pallas kernels for 0% -> 0%
where the time goes in v1:
time: 53.2 us; the launch traced here: 52.9 us
  Pallas kernels  42.3 us (80%)
  local copies, waits for them, and re-layouts  9.94 us (19%)
  between operations  0.65 us (1%)
    pallas_call x1, Pallas kernels, local(): pl.pallas_call(functools.partial(kernel, n, nr, ns), out_shape=(jax.Shape...  42.3 us
    unnamed x17, local copies, waits for them, and re-layouts  9.94 us

profile of v1, /device:TPU:0, one launch (start us, length us, event | category | flops | bytes accessed | tf_op | source)
XLA Modules:
  0.0 52.9 jit_solution(16009057500948570227)
XLA Ops:
  0.6 0.8 %copy.11.scale = f32[16,8]{1,0:T(8,128)S(1)} copy(f32[16,8]{0,1:T(8,128)} %param.8) | data formatting | bytes 1024 | tf_op args[1]
  1.4 0.0 copy-start
  1.4 2.2 %copy-done = bf16[2048,1024]{1,0:T(8,128)(2,1)S(1)} copy-done((bf16[2048,1024]{1,0:T(8,128)(2,1)S(1)}, bf16[2048,1024]{1,0:T(8,128)(2,1)}, u32[]{:S(2)}) %copy-start) | copy-done | bytes 4194328
  3.6 0.0 copy-start.1
  3.6 1.0 %copy-done.1 = f32[64,2048]{1,0:T(8,128)S(1)} copy-done((f32[64,2048]{1,0:T(8,128)S(1)}, f32[64,2048]{1,0:T(8,128)}, u32[]{:S(2)}) %copy-start.1) | copy-done | bytes 524312
  4.6 0.0 copy-start.2
  4.6 0.9 %copy-done.2 = f32[64,1024]{1,0:T(8,128)S(1)} copy-done((f32[64,1024]{1,0:T(8,128)S(1)}, f32[64,1024]{1,0:T(8,128)}, u32[]{:S(2)}) %copy-start.2) | copy-done | bytes 262168
  5.6 0.0 copy-start.3
  5.6 0.9 %copy-done.3 = f32[64,1024]{1,0:T(8,128)S(1)} copy-done((f32[64,1024]{1,0:T(8,128)S(1)}, f32[64,1024]{1,0:T(8,128)}, u32[]{:S(2)}) %copy-start.3) | copy-done | bytes 262168
  6.5 0.0 copy-start.4
  6.5 0.7 %copy-done.4 = f32[1024]{0:T(1024)S(1)} copy-done((f32[1024]{0:T(1024)S(1)}, f32[1024]{0:T(1024)}, u32[]{:S(2)}) %copy-start.4) | copy-done | bytes 4120
  7.2 0.0 copy-start.5
  7.2 0.7 %copy-done.5 = f32[64]{0:T(128)S(1)} copy-done((f32[64]{0:T(128)S(1)}, f32[64]{0:T(128)}, u32[]{:S(2)}) %copy-start.5) | copy-done | bytes 280
  7.9 42.3 %cgls_iteration.1 = (f32[64,1024]{1,0:T(8,128)S(1)}, f32[64,2048]{1,0:T(8,128)S(1)}, f32[64,1024]{1,0:T(8,128)S(1)}, f32[64]{0:T(128)S(1)}) custom-call(bf16[2048,1024]{1,0:T(8,128)(2,1)S(1)} %copy-done, f32[16,8]{1,0:T(8,128)S(1)} %copy.11.scale, f32[1024]{0:T(1024)S(1)} %copy-done.4, f32[64,1024]{1,0:T(8,128)S(1)} %copy-done.2, f32[64,2048]{1,0:T(8,128)S(1)} %copy-done.1, ...), custom_call_target="tpu_custom_call" | custom-call | flops 536870912 | bytes 4194304 | tf_op jit(solution)/shard_map/cgls_iteration/pallas_call | solution.py:301
  50.2 0.7 %copy.16 = f32[64,1024]{1,0:T(8,128)} copy(f32[64,1024]{1,0:T(8,128)S(1)} %get-tuple-element.8) | data formatting | bytes 524288
  50.9 0.8 %copy.17 = f32[64,2048]{1,0:T(8,128)} copy(f32[64,2048]{1,0:T(8,128)S(1)} %get-tuple-element.9) | data formatting | bytes 1048576
  51.7 0.7 %copy.18 = f32[64,1024]{1,0:T(8,128)} copy(f32[64,1024]{1,0:T(8,128)S(1)} %get-tuple-element.10) | data formatting | bytes 524288
  52.4 0.5 copy.19
Async XLA Ops:
  1.4 2.2 %copy-start = (bf16[2048,1024]{1,0:T(8,128)(2,1)S(1)}, bf16[2048,1024]{1,0:T(8,128)(2,1)}, u32[]{:S(2)}) copy-start(bf16[2048,1024]{1,0:T(8,128)(2,1)} %sens_hbm.1) | copy-start | bytes 12582916
  3.6 1.0 %copy-start.1 = (f32[64,2048]{1,0:T(8,128)S(1)}, f32[64,2048]{1,0:T(8,128)}, u32[]{:S(2)}) copy-start(f32[64,2048]{1,0:T(8,128)} %resid_hbm.1) | copy-start | bytes 1572868
  4.6 0.9 %copy-start.2 = (f32[64,1024]{1,0:T(8,128)S(1)}, f32[64,1024]{1,0:T(8,128)}, u32[]{:S(2)}) copy-start(f32[64,1024]{1,0:T(8,128)} %model_hbm.1) | copy-start | bytes 786436
  5.6 0.9 %copy-start.3 = (f32[64,1024]{1,0:T(8,128)S(1)}, f32[64,1024]{1,0:T(8,128)}, u32[]{:S(2)}) copy-start(f32[64,1024]{1,0:T(8,128)} %direc_hbm.1) | copy-start | bytes 786436
  6.5 0.7 %copy-start.4 = (f32[1024]{0:T(1024)S(1)}, f32[1024]{0:T(1024)}, u32[]{:S(2)}) copy-start(f32[1024]{0:T(1024)} %depth.1) | copy-start | bytes 12292
  7.2 0.7 %copy-start.5 = (f32[64]{0:T(128)S(1)}, f32[64]{0:T(128)}, u32[]{:S(2)}) copy-start(f32[64]{0:T(128)} %gamma.1) | copy-start | bytes 772

commit v2 on v1

--- a/solution.py
+++ b/solution.py
@@ -28,10 +28,10 @@
 
 def kernel(
     n, nr, ns,
-    sens_hbm, scale, depth, model_hbm, resid_hbm, direc_hbm, gamma,
-    model_out, resid_out, direc_out, gamma_out,
-    sens, model, resid, direc, scaled, part, recv, pred, curv, grad, other, gams,
-    sens_sem, load_sem, out_sem,
+    sens_hbm, scale_hbm, depth_hbm, model_hbm, resid_hbm, direc_hbm, gamma_hbm,
+    model, resid, direc, grad, small,
+    scale, depth, gamma, sens, scaled, part, recv, pred, curv, other, gams,
+    sens_sem, load_sem,
     rs_send, rs_recv, ag_send, ag_recv, cv_send, cv_recv, dp_send, dp_recv, gm_send, gm_recv,
 ):
     sets, cells = direc.shape
@@ -55,6 +55,12 @@
 
     direc_load = pltpu.make_async_copy(direc_hbm, direc, load_sem.at[0])
     direc_load.start()
+    depth_load = pltpu.make_async_copy(depth_hbm, depth, load_sem.at[3])
+    depth_load.start()
+    scale_load = pltpu.make_async_copy(scale_hbm, scale, load_sem.at[4])
+    scale_load.start()
+    gamma_load = pltpu.make_async_copy(gamma_hbm, gamma, load_sem.at[5])
+    gamma_load.start()
     for t in range(nr):
         sens_copy(t).start()
     resid_load = pltpu.make_async_copy(resid_hbm, resid, load_sem.at[1])
@@ -73,6 +79,9 @@
 
     lax.fori_loop(1, total, greet, 0)
 
+    depth_load.wait()
+    gamma_load.wait()
+    scale_load.wait()
     inverse = 1.0 / depth[...].reshape(1, cells)
     gamma_row = jnp.concatenate(
         [gamma[...].reshape(1, sets), jnp.ones((1, 128 - sets), jnp.float32)], axis=1
@@ -104,7 +113,7 @@
                 preferred_element_type=jnp.float32,
             )
             for a in range(row_blocks):
-                term = tile[:, a * BLOCK:(a + 1) * BLOCK] * scale[q * row_blocks + a, b]
+                term = tile[:, a * BLOCK:(a + 1) * BLOCK] * scale[b, q * row_blocks + a]
                 accs[a] = term if accs[a] is None else accs[a] + term
         for a in range(row_blocks):
             part[q, :, a * BLOCK:(a + 1) * BLOCK] = accs[a]
@@ -180,8 +189,6 @@
 
     model_load.wait()
     model[...] = model[...] + step * direc[...]
-    model_store = pltpu.make_async_copy(model, model_out, out_sem.at[0])
-    model_store.start()
     resid_load.wait()
     grad[...] = jnp.zeros(grad.shape, jnp.float32)
 
@@ -211,7 +218,7 @@
                 acc = acc + jnp.concatenate(
                     [
                         tile[:, b * BLOCK:(b + 1) * BLOCK]
-                        * scale[q * row_blocks + a, p * (width // BLOCK) + b]
+                        * scale[p * (width // BLOCK) + b, q * row_blocks + a]
                         for b in range(width // BLOCK)
                     ],
                     axis=1,
@@ -229,8 +236,6 @@
 
     for p in range(pieces):
         dp_copy(p).start()
-    resid_store = pltpu.make_async_copy(resid, resid_out, out_sem.at[1])
-    resid_store.start()
 
     square = jnp.zeros((sets, 1), jnp.float32)
     for p in range(pieces):
@@ -260,13 +265,8 @@
     gamma_new = lax.fori_loop(
         0, n, lambda i, acc: acc + gams[i], jnp.zeros((1, 128), jnp.float32)
     )
-    gamma_out[...] = gamma_new[:, :sets].reshape(sets)
-    ratio = to_column(gamma_new / gamma_row, sets)
-    for p in range(pieces):
-        span = slice(p * width, (p + 1) * width)
-        direc[:, span] = grad[p] + ratio * direc[:, span]
-    direc_store = pltpu.make_async_copy(direc, direc_out, out_sem.at[2])
-    direc_store.start()
+    small[0:1, :] = gamma_new
+    small[1:2, :] = gamma_new / gamma_row
 
     def drain(t, _):
         peer = lax.rem(me + t, n)
@@ -281,9 +281,27 @@
 
     lax.fori_loop(1, n, drain, 0)
     lax.fori_loop(1, total, cv_drain, 0)
-    model_store.wait()
-    resid_store.wait()
-    direc_store.wait()
+
+
+def finish(model, resid, direc, grad, small, model_out, resid_out, direc_out, gamma_out, fresh, sem):
+    sets = direc.shape[0]
+    pieces, _, width = grad.shape
+    copies = [
+        pltpu.make_async_copy(model, model_out, sem.at[0]),
+        pltpu.make_async_copy(resid, resid_out, sem.at[1]),
+    ]
+    for copy in copies:
+        copy.start()
+    ratio = to_column(small[1:2, :], sets)
+    for p in range(pieces):
+        span = slice(p * width, (p + 1) * width)
+        fresh[:, span] = grad[p] + ratio * direc[:, span]
+    last = pltpu.make_async_copy(fresh, direc_out, sem.at[2])
+    last.start()
+    gamma_out[...] = small[0, :sets]
+    for copy in copies:
+        copy.wait()
+    last.wait()
 
 
 def local(n, sensitivity, block_scale, depth_weight, model, residual, direction, gamma):
@@ -294,46 +312,59 @@
     cr, cs = rows // nr, sets // ns
     pieces = 4
     f32 = jnp.float32
-    any_space = pl.BlockSpec(memory_space=pl.ANY)
+    hbm = pl.BlockSpec(memory_space=pltpu.HBM)
     vmem = pl.BlockSpec(memory_space=pltpu.VMEM)
-    smem = pl.BlockSpec(memory_space=pltpu.SMEM)
     dma = pltpu.SemaphoreType.DMA
+    parts = pl.pallas_call(
+        functools.partial(kernel, n, nr, ns),
+        out_shape=(
+            pltpu.VMEM(model.shape, f32),
+            pltpu.VMEM(residual.shape, f32),
+            pltpu.VMEM(direction.shape, f32),
+            pltpu.VMEM((pieces, sets, cells // pieces), f32),
+            pltpu.VMEM((8, 128), f32),
+        ),
+        in_specs=[hbm] * 7,
+        out_specs=(vmem,) * 5,
+        scratch_shapes=[
+            pltpu.SMEM(block_scale.shape[::-1], f32),
+            pltpu.VMEM(depth_weight.shape, f32),
+            pltpu.VMEM(gamma.shape, f32),
+            pltpu.VMEM((nr, cr, cells), jnp.bfloat16),
+            pltpu.VMEM((sets, cells), jnp.bfloat16),
+            pltpu.VMEM((nr, sets, cr), f32),
+            pltpu.VMEM((n, cs, cr), f32),
+            pltpu.VMEM((nr, sets, cr), f32),
+            pltpu.VMEM((2 * n, 1, 128), f32),
+            pltpu.VMEM((pieces, sets, cells // pieces), f32),
+            pltpu.VMEM((n, 1, 128), f32),
+            dma((nr,)), dma((6,)),
+            dma((n,)), dma((n,)), dma((n,)), dma((n,)),
+            dma((2 * n,)), dma((2 * n,)), dma((pieces,)), dma((pieces,)),
+            dma((n,)), dma((n,)),
+        ],
+        compiler_params=pltpu.CompilerParams(
+            collective_id=0, has_side_effects=True, vmem_limit_bytes=56 * 1024 * 1024
+        ),
+        cost_estimate=pl.CostEstimate(
+            flops=4 * rows * cells * sets, bytes_accessed=2 * rows * cells, transcendentals=0
+        ),
+        name="cgls_iteration",
+    )(sensitivity, block_scale.T, depth_weight, model, residual, direction, gamma)
     return pl.pallas_call(
-        functools.partial(kernel, n, nr, ns),
+        finish,
         out_shape=(
             jax.ShapeDtypeStruct(model.shape, f32),
             jax.ShapeDtypeStruct(residual.shape, f32),
             jax.ShapeDtypeStruct(direction.shape, f32),
             jax.ShapeDtypeStruct(gamma.shape, f32),
         ),
-        in_specs=[any_space, smem, vmem, any_space, any_space, any_space, vmem],
-        out_specs=(any_space, any_space, any_space, vmem),
-        scratch_shapes=[
-            pltpu.VMEM((nr, cr, cells), jnp.bfloat16),
-            pltpu.VMEM((sets, cells), f32),
-            pltpu.VMEM((sets, rows), f32),
-            pltpu.VMEM((sets, cells), f32),
-            pltpu.VMEM((sets, cells), jnp.bfloat16),
-            pltpu.VMEM((nr, sets, cr), f32),
-            pltpu.VMEM((n, cs, cr), f32),
-            pltpu.VMEM((nr, sets, cr), f32),
-            pltpu.VMEM((2 * n, 1, 128), f32),
-            pltpu.VMEM((pieces, sets, cells // pieces), f32),
-            pltpu.VMEM((pieces, sets, cells // pieces), f32),
-            pltpu.VMEM((n, 1, 128), f32),
-            dma((nr,)), dma((3,)), dma((3,)),
-            dma((n,)), dma((n,)), dma((n,)), dma((n,)),
-            dma((2 * n,)), dma((2 * n,)), dma((pieces,)), dma((pieces,)),
-            dma((n,)), dma((n,)),
-        ],
-        compiler_params=pltpu.CompilerParams(
-            collective_id=0, has_side_effects=True, vmem_limit_bytes=32 * 1024 * 1024
-        ),
-        cost_estimate=pl.CostEstimate(
-            flops=4 * rows * cells * sets, bytes_accessed=2 * rows * cells, transcendentals=0
-        ),
-        name="cgls_iteration",
-    )(sensitivity, block_scale, depth_weight, model, residual, direction, gamma)
+        in_specs=[vmem] * 5,
+        out_specs=(hbm, hbm, hbm, vmem),
+        scratch_shapes=[pltpu.VMEM(direction.shape, f32), dma((3,))],
+        compiler_params=pltpu.CompilerParams(vmem_limit_bytes=16 * 1024 * 1024),
+        name="cgls_results",
+    )(*parts)
 
 
 def solution(mesh):

time: 53.2 us -> 43.5 us (0.82)
  local copies, waits for them, and re-layouts: 9.94 us -> 0 us
    unnamed x17 -> x0, local copies, waits for them, and re-layouts: 9.94 us -> none
    pallas_call x1 -> x2, Pallas kernels: 42.3 us -> 42.7 us  [the longest x1 41.2 us: local(): pl.pallas_call(functools.partial(kernel, n, nr, ns), out_shape=(pltpu.VME...]
where the time goes in v2:
time: 43.5 us; the launch traced here: 43.3 us
  Pallas kernels  42.7 us (98%)
  between operations  0.64 us (1%)
    pallas_call x1, Pallas kernels, local(): pl.pallas_call(functools.partial(kernel, n, nr, ns), out_shape=(pltpu.VME...  41.2 us
    pallas_call x1, Pallas kernels, local(): pl.pallas_call(finish, out_shape=(jax.ShapeDtypeStruct(model.shape, f32),...  1.5 us

profile of v2, /device:TPU:0, one launch (start us, length us, event | category | flops | bytes accessed | tf_op | source)
XLA Modules:
  0.0 43.3 jit_solution(8020268461509717424)
XLA Ops:
  0.6 41.2 %cgls_iteration.1 = (f32[64,1024]{1,0:T(8,128)S(1)}, f32[64,2048]{1,0:T(8,128)S(1)}, f32[64,1024]{1,0:T(8,128)S(1)}, f32[4,64,256]{2,1,0:T(8,128)S(1)}, f32[8,128]{1,0:T(8,128)S(1)}) custom-call(bf16[2048,1024]{1,0:T(8,128)(2,1)} %sens_hbm.1, f32[8,16]{1,0:T(8,128)} %bitcast.1, f32[1024]{0:T(1024)} %depth_hbm.1, f32[64,1024]{1,0:T(8,128)} %model_hbm.1, ...), custom_call_target="tpu_custom_call" | custom-call | flops 536870912 | bytes 4194304 | tf_op jit(solution)/shard_map/cgls_iteration/pallas_call | solution.py:318
  41.8 1.5 %cgls_results.1 = (f32[64,1024]{1,0:T(8,128)}, f32[64,2048]{1,0:T(8,128)}, f32[64,1024]{1,0:T(8,128)}, f32[64]{0:T(128)}) custom-call(f32[64,1024]{1,0:T(8,128)S(1)} %get-tuple-element.9.model, f32[64,2048]{1,0:T(8,128)S(1)} %get-tuple-element.10.resid, f32[64,1024]{1,0:T(8,128)S(1)} %get-tuple-element.11.direc, f32[4,64,256]{2,1,0:T(8,128)S(1)} %get-tuple-element.12.grad, ...), custom_call_target="tpu_custom_call" | custom-call | tf_op jit(solution)/shard_map/cgls_results/pallas_call | solution.py:354

commit v3 on v2

--- a/solution.py
+++ b/solution.py
@@ -27,15 +27,17 @@
 
 
 def kernel(
-    n, nr, ns,
+    n, nr, ns, fa, ga,
     sens_hbm, scale_hbm, depth_hbm, model_hbm, resid_hbm, direc_hbm, gamma_hbm,
     model, resid, direc, grad, small,
-    scale, depth, gamma, sens, scaled, part, recv, pred, curv, other, gams,
-    sens_sem, load_sem,
+    scale, depth, gamma, sens, scaled, part, recv, xin, zin, pred, curv, other, gams,
+    sens_sem, load_sem, x_send, x_recv, z_send, z_recv, ax_send, ax_recv, az_send, az_recv,
     rs_send, rs_recv, ag_send, ag_recv, cv_send, cv_recv, dp_send, dp_recv, gm_send, gm_recv,
 ):
     sets, cells = direc.shape
-    cs, cr = recv.shape[1:]
+    cs, cr = sets // ns, recv.shape[2]
+    paired = fa > 0
+    nz = n // 2
     row_blocks = cr // BLOCK
     col_blocks = cells // BLOCK
     pieces = grad.shape[0]
@@ -46,9 +48,17 @@
     rank = me * 2 + core
     my_q = me // ns
     my_g = me % ns
+    x = lax.rem(me, 2)
+    z = me // 2
+    beside = 2 * z + 1 - x
+
+    def chunk_at(t):
+        if not paired:
+            return lax.rem(my_q + 1 + t, nr)
+        return 2 * lax.rem(z + 1 + t, nz) + lax.rem(x + 1 + t // nz, 2)
 
     def sens_copy(t):
-        q = lax.rem(my_q + 1 + t, nr)
+        q = chunk_at(t)
         return pltpu.make_async_copy(
             sens_hbm.at[pl.ds(pl.multiple_of(q * cr, cr), cr), :], sens.at[t], sens_sem.at[t]
         )
@@ -93,7 +103,7 @@
     def rs_copy(q, g):
         j = q * ns + g
         return pltpu.make_async_remote_copy(
-            src_ref=part.at[q, pl.ds(pl.multiple_of(g * cs, cs), cs), :],
+            src_ref=part.at[q, pl.ds(pl.multiple_of(g * cs + fa, 8), cs - fa), :],
             dst_ref=recv.at[me],
             send_sem=rs_send.at[j],
             recv_sem=rs_recv.at[me],
@@ -101,8 +111,8 @@
             device_id_type=MESH,
         )
 
-    def forward(t, _):
-        q = lax.rem(my_q + 1 + t, nr)
+    def forward(t):
+        q = chunk_at(t)
         sens_copy(t).wait()
         accs = [None] * row_blocks
         for b in range(col_blocks):
@@ -117,19 +127,61 @@
                 accs[a] = term if accs[a] is None else accs[a] + term
         for a in range(row_blocks):
             part[q, :, a * BLOCK:(a + 1) * BLOCK] = accs[a]
-
-        def send(g, _):
-            @pl.when(q * ns + g != me)
-            def _():
-                rs_copy(q, g).start()
-            return 0
-
-        lax.fori_loop(0, ns, send, 0)
-        return 0
-
-    lax.fori_loop(0, nr, forward, 0)
-
-    mine = pl.ds(pl.multiple_of(my_g * cs, cs), cs)
+        return q
+
+    def x_copy(zz):
+        return pltpu.make_async_remote_copy(
+            src_ref=part.at[2 * zz + 1 - x, pl.ds(0, fa), :], dst_ref=xin.at[zz],
+            send_sem=x_send.at[zz], recv_sem=x_recv.at[zz],
+            device_id={"cell": beside}, device_id_type=MESH,
+        )
+
+    def z_copy(slot, zz):
+        return pltpu.make_async_remote_copy(
+            src_ref=part.at[2 * zz + x, pl.ds(0, fa), :], dst_ref=zin.at[slot],
+            send_sem=z_send.at[zz], recv_sem=z_recv.at[slot],
+            device_id={"cell": 2 * zz + x}, device_id_type=MESH,
+        )
+
+    if paired:
+        def across(t, _):
+            q = forward(t)
+            x_copy(q // 2).start()
+            rs_copy(q, 0).start()
+            return 0
+
+        def along(t, _):
+            rs_copy(forward(t), 0).start()
+            return 0
+
+        def pass_on(t, _):
+            zz = lax.rem(z + 1 + t, nz)
+            x_copy(zz).wait_recv()
+            part[2 * zz + x, :fa, :] += xin[zz]
+            z_copy(z, zz).start()
+            return 0
+
+        lax.fori_loop(0, nz, across, 0)
+        lax.fori_loop(nz, n - 1, along, 0)
+        forward(n - 1)
+        lax.fori_loop(0, nz - 1, pass_on, 0)
+    else:
+        def spread(t, _):
+            q = forward(t)
+
+            def send(g, _):
+                @pl.when(q * ns + g != me)
+                def _():
+                    rs_copy(q, g).start()
+                return 0
+
+            lax.fori_loop(0, ns, send, 0)
+            return 0
+
+        lax.fori_loop(0, nr, spread, 0)
+
+    mine = pl.ds(pl.multiple_of(my_g * cs, 8), cs)
+    direct = pl.ds(pl.multiple_of(my_g * cs + fa, 8), cs - fa)
 
     def rs_arrival(src):
         return pltpu.make_async_remote_copy(
@@ -142,10 +194,22 @@
     def reduce(t, _):
         src = lax.rem(me + t, n)
         rs_arrival(src).wait_recv()
-        pred[my_q, mine, :] += recv[src]
+        pred[my_q, direct, :] += recv[src]
         return 0
 
     lax.fori_loop(1, n, reduce, 0)
+
+    if paired:
+        x_copy(z).wait_recv()
+        pred[me, :fa, :] += xin[z]
+
+        def reduce_z(t, _):
+            zz = lax.rem(z + t, nz)
+            z_copy(zz, zz).wait_recv()
+            pred[me, :fa, :] += zin[zz]
+            return 0
+
+        lax.fori_loop(1, nz, reduce_z, 0)
 
     value = pred[my_q, mine, :]
     curv[rank] = to_row(jnp.sum(value * value, axis=1, keepdims=True), my_g * cs)
@@ -164,17 +228,46 @@
     lax.fori_loop(1, total, cv_start, 0)
 
     def ag_copy(q, g, peer):
-        ref = pred.at[q, pl.ds(pl.multiple_of(g * cs, cs), cs), :]
+        ref = pred.at[q, pl.ds(pl.multiple_of(g * cs + ga, 8), cs - ga), :]
         return pltpu.make_async_remote_copy(
             src_ref=ref, dst_ref=ref, send_sem=ag_send.at[peer],
             recv_sem=ag_recv.at[q * ns + g], device_id={"cell": peer}, device_id_type=MESH,
         )
 
-    def ag_start(t, _):
-        ag_copy(my_q, my_g, lax.rem(me + t, n)).start()
-        return 0
-
-    lax.fori_loop(1, n, ag_start, 0)
+    def az_copy(owner, zz):
+        ref = pred.at[owner, pl.ds(0, ga), :]
+        return pltpu.make_async_remote_copy(
+            src_ref=ref, dst_ref=ref, send_sem=az_send.at[zz], recv_sem=az_recv.at[owner // 2],
+            device_id={"cell": 2 * zz + x}, device_id_type=MESH,
+        )
+
+    def ax_copy(owner):
+        ref = pred.at[owner, pl.ds(0, ga), :]
+        return pltpu.make_async_remote_copy(
+            src_ref=ref, dst_ref=ref, send_sem=ax_send.at[owner // 2],
+            recv_sem=ax_recv.at[owner // 2], device_id={"cell": beside}, device_id_type=MESH,
+        )
+
+    if paired:
+        for t in range(1, nz):
+            az_copy(me, lax.rem(z + t, nz)).start()
+        ax_copy(me).start()
+        for t in range(1, nz):
+            az_copy(me, lax.rem(z + t, nz)).wait_send()
+        for t in range(1, nz):
+            ag_copy(me, 0, 2 * lax.rem(z + t, nz) + x).start()
+        for t in range(nz):
+            ag_copy(me, 0, 2 * lax.rem(z + t, nz) + 1 - x).start()
+        for t in range(1, nz):
+            zz = lax.rem(z + nz - t, nz)
+            az_copy(2 * zz + x, zz).wait_recv()
+            ax_copy(2 * zz + x).start()
+    else:
+        def ag_start(t, _):
+            ag_copy(my_q, my_g, lax.rem(me + t, n)).start()
+            return 0
+
+        lax.fori_loop(1, n, ag_start, 0)
 
     def cv_wait(t, _):
         peer = lax.rem(rank + t, total)
@@ -192,9 +285,14 @@
     resid_load.wait()
     grad[...] = jnp.zeros(grad.shape, jnp.float32)
 
-    def backward(u, _):
-        t = nr - 1 - u
-        q = lax.rem(my_q + 1 + t, nr)
+    def dp_copy(p):
+        return pltpu.make_async_remote_copy(
+            src_ref=grad.at[p], dst_ref=other.at[p], send_sem=dp_send.at[p],
+            recv_sem=dp_recv.at[p], device_id={"dp": 1 - core}, device_id_type=MESH,
+        )
+
+    def backward(t, last):
+        q = chunk_at(t)
 
         def arrive(g, _):
             @pl.when(q * ns + g != me)
@@ -202,7 +300,10 @@
                 ag_copy(q, g, q * ns + g).wait_recv()
             return 0
 
-        lax.fori_loop(0, ns, arrive, 0)
+        if not last or not paired:
+            lax.fori_loop(0, ns, arrive, 0)
+        else:
+            ag_copy(q, 0, q).wait_recv()
         where = pl.ds(pl.multiple_of(q * cr, cr), cr)
         fresh = resid[:, where] - step * pred[q]
         resid[:, where] = fresh
@@ -224,18 +325,26 @@
                     axis=1,
                 )
             grad[p] = acc
-        return 0
-
-    lax.fori_loop(0, nr, backward, 0)
-
-    def dp_copy(p):
-        return pltpu.make_async_remote_copy(
-            src_ref=grad.at[p], dst_ref=other.at[p], send_sem=dp_send.at[p],
-            recv_sem=dp_recv.at[p], device_id={"dp": 1 - core}, device_id_type=MESH,
-        )
-
-    for p in range(pieces):
-        dp_copy(p).start()
+            if last:
+                dp_copy(p).start()
+
+    def own_column(u, _):
+        backward(nr - 1 - u, False)
+        return 0
+
+    def other_column(u, _):
+        t = nr - 1 - u
+        ax_copy(2 * (chunk_at(t) // 2) + x).wait_recv()
+        backward(t, False)
+        return 0
+
+    if paired:
+        lax.fori_loop(0, nz, own_column, 0)
+        lax.fori_loop(nz, nr - 1, other_column, 0)
+        ax_copy(2 * (chunk_at(0) // 2) + x).wait_recv()
+    else:
+        lax.fori_loop(0, nr - 1, own_column, 0)
+    backward(0, True)
 
     square = jnp.zeros((sets, 1), jnp.float32)
     for p in range(pieces):
@@ -274,6 +383,13 @@
         ag_copy(my_q, my_g, peer).wait_send()
         gm_copy(me, peer).wait_send()
         return 0
+
+    if paired:
+        for zz in range(nz):
+            x_copy(zz).wait_send()
+            ax_copy(2 * zz + x).wait_send()
+        for t in range(1, nz):
+            z_copy(z, lax.rem(z + t, nz)).wait_send()
 
     def cv_drain(t, _):
         cv_copy(rank, lax.rem(rank + t, total)).wait_send()
@@ -310,13 +426,16 @@
     nr = min(n, rows // BLOCK)
     ns = n // nr
     cr, cs = rows // nr, sets // ns
+    paired = ns == 1 and n % 2 == 0 and n > 2 and cs >= 32
+    fa, ga = (cs * 3 // 4 // 8 * 8, cs // 2 // 8 * 8) if paired else (0, 0)
+    nz, kept = (n // 2, fa) if paired else (1, 8)
     pieces = 4
     f32 = jnp.float32
     hbm = pl.BlockSpec(memory_space=pltpu.HBM)
     vmem = pl.BlockSpec(memory_space=pltpu.VMEM)
     dma = pltpu.SemaphoreType.DMA
     parts = pl.pallas_call(
-        functools.partial(kernel, n, nr, ns),
+        functools.partial(kernel, n, nr, ns, fa, ga),
         out_shape=(
             pltpu.VMEM(model.shape, f32),
             pltpu.VMEM(residual.shape, f32),
@@ -333,12 +452,16 @@
             pltpu.VMEM((nr, cr, cells), jnp.bfloat16),
             pltpu.VMEM((sets, cells), jnp.bfloat16),
             pltpu.VMEM((nr, sets, cr), f32),
-            pltpu.VMEM((n, cs, cr), f32),
+            pltpu.VMEM((n, cs - fa, cr), f32),
+            pltpu.VMEM((nz, kept, cr), f32),
+            pltpu.VMEM((nz, kept, cr), f32),
             pltpu.VMEM((nr, sets, cr), f32),
             pltpu.VMEM((2 * n, 1, 128), f32),
             pltpu.VMEM((pieces, sets, cells // pieces), f32),
             pltpu.VMEM((n, 1, 128), f32),
             dma((nr,)), dma((6,)),
+            dma((nz,)), dma((nz,)), dma((nz,)), dma((nz,)),
+            dma((nz,)), dma((nz,)), dma((nz,)), dma((nz,)),
             dma((n,)), dma((n,)), dma((n,)), dma((n,)),
             dma((2 * n,)), dma((2 * n,)), dma((pieces,)), dma((pieces,)),
             dma((n,)), dma((n,)),

time: 43.5 us -> 35.8 us (0.82)
  Pallas kernels: 42.7 us -> 35 us
    pallas_call x1, Pallas kernels: 41.2 us -> 33.5 us  [local(): pl.pallas_call(functools.partial(kernel, n, nr, ns, fa, ga), out_shape=(p...]
where the time goes in v3:
time: 35.8 us; the launch traced here: 35.7 us
  Pallas kernels  35 us (98%)
  between operations  0.64 us (2%)
    pallas_call x1, Pallas kernels, local(): pl.pallas_call(functools.partial(kernel, n, nr, ns, fa, ga), out_shape=(p...  33.5 us
    pallas_call x1, Pallas kernels, local(): pl.pallas_call(finish, out_shape=(jax.ShapeDtypeStruct(model.shape, f32),...  1.5 us

profile of v3, /device:TPU:0, one launch (start us, length us, event | category | flops | bytes accessed | tf_op | source)
XLA Modules:
  0.0 35.7 jit_solution(3972335857938918088)
XLA Ops:
  0.6 33.5 %cgls_iteration.1 = (f32[64,1024]{1,0:T(8,128)S(1)}, f32[64,2048]{1,0:T(8,128)S(1)}, f32[64,1024]{1,0:T(8,128)S(1)}, f32[4,64,256]{2,1,0:T(8,128)S(1)}, f32[8,128]{1,0:T(8,128)S(1)}) custom-call(bf16[2048,1024]{1,0:T(8,128)(2,1)} %sens_hbm.1, f32[8,16]{1,0:T(8,128)} %bitcast.1, f32[1024]{0:T(1024)} %depth_hbm.1, f32[64,1024]{1,0:T(8,128)} %model_hbm.1, ...), custom_call_target="tpu_custom_call" | custom-call | flops 536870912 | bytes 4194304 | tf_op jit(solution)/shard_map/cgls_iteration/pallas_call | solution.py:437
  34.2 1.5 %cgls_results.1 = (f32[64,1024]{1,0:T(8,128)}, f32[64,2048]{1,0:T(8,128)}, f32[64,1024]{1,0:T(8,128)}, f32[64]{0:T(128)}) custom-call(f32[64,1024]{1,0:T(8,128)S(1)} %get-tuple-element.9.model, f32[64,2048]{1,0:T(8,128)S(1)} %get-tuple-element.10.resid, f32[64,1024]{1,0:T(8,128)S(1)} %get-tuple-element.11.direc, f32[4,64,256]{2,1,0:T(8,128)S(1)} %get-tuple-element.12.grad, ...), custom_call_target="tpu_custom_call" | custom-call | tf_op jit(solution)/shard_map/cgls_results/pallas_call | solution.py:477

commit v4 on v3

--- a/solution.py
+++ b/solution.py
@@ -87,7 +87,7 @@
         )
         return 0
 
-    lax.fori_loop(1, total, greet, 0)
+    lax.fori_loop(1, total, greet, 0, unroll=n <= 8)
 
     depth_load.wait()
     gamma_load.wait()
@@ -98,7 +98,6 @@
     )
     direc_load.wait()
     scaled[...] = (direc[...] * inverse).astype(jnp.bfloat16)
-    pl.semaphore_wait(barrier, total - 1)
 
     def rs_copy(q, g):
         j = q * ns + g
@@ -146,6 +145,11 @@
     if paired:
         def across(t, _):
             q = forward(t)
+
+            @pl.when(t == 0)
+            def _():
+                pl.semaphore_wait(barrier, total - 1)
+
             x_copy(q // 2).start()
             rs_copy(q, 0).start()
             return 0
@@ -164,8 +168,10 @@
         lax.fori_loop(0, nz, across, 0)
         lax.fori_loop(nz, n - 1, along, 0)
         forward(n - 1)
-        lax.fori_loop(0, nz - 1, pass_on, 0)
+        lax.fori_loop(0, nz - 1, pass_on, 0, unroll=n <= 8)
     else:
+        pl.semaphore_wait(barrier, total - 1)
+
         def spread(t, _):
             q = forward(t)
 
@@ -189,6 +195,41 @@
             recv_sem=rs_recv.at[src], device_id={"cell": src}, device_id_type=MESH,
         )
 
+    relayed = (pl.ds(0, max(ga, 8)), pl.ds(fa, cs - fa))
+    top = fa if paired else cs
+
+    def ag_copy(q, g, peer):
+        ref = pred.at[q, pl.ds(pl.multiple_of(g * cs + ga, 8), top - ga), :]
+        return pltpu.make_async_remote_copy(
+            src_ref=ref, dst_ref=ref, send_sem=ag_send.at[peer],
+            recv_sem=ag_recv.at[q * ns + g], device_id={"cell": peer}, device_id_type=MESH,
+        )
+
+    def az_copy(k, owner, zz):
+        ref = pred.at[owner, relayed[k], :]
+        return pltpu.make_async_remote_copy(
+            src_ref=ref, dst_ref=ref, send_sem=az_send.at[k, zz], recv_sem=az_recv.at[k, owner // 2],
+            device_id={"cell": 2 * zz + x}, device_id_type=MESH,
+        )
+
+    def ax_copy(k, owner):
+        ref = pred.at[owner, relayed[k], :]
+        return pltpu.make_async_remote_copy(
+            src_ref=ref, dst_ref=ref, send_sem=ax_send.at[k, owner // 2],
+            recv_sem=ax_recv.at[k, owner // 2], device_id={"cell": beside}, device_id_type=MESH,
+        )
+
+    def relay_start(k):
+        for t in range(1, nz):
+            az_copy(k, me, lax.rem(z + t, nz)).start()
+        ax_copy(k, me).start()
+
+    def relay(k):
+        for t in range(1, nz):
+            zz = lax.rem(z + nz - t, nz)
+            az_copy(k, 2 * zz + x, zz).wait_recv()
+            ax_copy(k, 2 * zz + x).start()
+
     pred[my_q, mine, :] = part[my_q, mine, :]
 
     def reduce(t, _):
@@ -197,9 +238,10 @@
         pred[my_q, direct, :] += recv[src]
         return 0
 
-    lax.fori_loop(1, n, reduce, 0)
+    lax.fori_loop(1, n, reduce, 0, unroll=n <= 8)
 
     if paired:
+        relay_start(1)
         x_copy(z).wait_recv()
         pred[me, :fa, :] += xin[z]
 
@@ -209,7 +251,11 @@
             pred[me, :fa, :] += zin[zz]
             return 0
 
-        lax.fori_loop(1, nz, reduce_z, 0)
+        lax.fori_loop(1, nz, reduce_z, 0, unroll=n <= 8)
+
+    if paired:
+        relay_start(0)
+        relay(1)
 
     value = pred[my_q, mine, :]
     curv[rank] = to_row(jnp.sum(value * value, axis=1, keepdims=True), my_g * cs)
@@ -225,43 +271,16 @@
         cv_copy(rank, lax.rem(rank + t, total)).start()
         return 0
 
-    lax.fori_loop(1, total, cv_start, 0)
-
-    def ag_copy(q, g, peer):
-        ref = pred.at[q, pl.ds(pl.multiple_of(g * cs + ga, 8), cs - ga), :]
-        return pltpu.make_async_remote_copy(
-            src_ref=ref, dst_ref=ref, send_sem=ag_send.at[peer],
-            recv_sem=ag_recv.at[q * ns + g], device_id={"cell": peer}, device_id_type=MESH,
-        )
-
-    def az_copy(owner, zz):
-        ref = pred.at[owner, pl.ds(0, ga), :]
-        return pltpu.make_async_remote_copy(
-            src_ref=ref, dst_ref=ref, send_sem=az_send.at[zz], recv_sem=az_recv.at[owner // 2],
-            device_id={"cell": 2 * zz + x}, device_id_type=MESH,
-        )
-
-    def ax_copy(owner):
-        ref = pred.at[owner, pl.ds(0, ga), :]
-        return pltpu.make_async_remote_copy(
-            src_ref=ref, dst_ref=ref, send_sem=ax_send.at[owner // 2],
-            recv_sem=ax_recv.at[owner // 2], device_id={"cell": beside}, device_id_type=MESH,
-        )
+    lax.fori_loop(1, total, cv_start, 0, unroll=n <= 8)
 
     if paired:
         for t in range(1, nz):
-            az_copy(me, lax.rem(z + t, nz)).start()
-        ax_copy(me).start()
-        for t in range(1, nz):
-            az_copy(me, lax.rem(z + t, nz)).wait_send()
+            az_copy(0, me, lax.rem(z + t, nz)).wait_send()
         for t in range(1, nz):
             ag_copy(me, 0, 2 * lax.rem(z + t, nz) + x).start()
         for t in range(nz):
             ag_copy(me, 0, 2 * lax.rem(z + t, nz) + 1 - x).start()
-        for t in range(1, nz):
-            zz = lax.rem(z + nz - t, nz)
-            az_copy(2 * zz + x, zz).wait_recv()
-            ax_copy(2 * zz + x).start()
+        relay(0)
     else:
         def ag_start(t, _):
             ag_copy(my_q, my_g, lax.rem(me + t, n)).start()
@@ -274,9 +293,9 @@
         cv_copy(peer, peer).wait_recv()
         return 0
 
-    lax.fori_loop(1, total, cv_wait, 0)
+    lax.fori_loop(1, total, cv_wait, 0, unroll=n <= 8)
     curvature = lax.fori_loop(
-        0, total, lambda i, acc: acc + curv[i], jnp.zeros((1, 128), jnp.float32)
+        0, total, lambda i, acc: acc + curv[i], jnp.zeros((1, 128), jnp.float32), unroll=n <= 8
     )
     step = to_column(gamma_row / (curvature + EPSILON), sets)
 
@@ -334,14 +353,16 @@
 
     def other_column(u, _):
         t = nr - 1 - u
-        ax_copy(2 * (chunk_at(t) // 2) + x).wait_recv()
+        for k in range(2):
+            ax_copy(k, 2 * (chunk_at(t) // 2) + x).wait_recv()
         backward(t, False)
         return 0
 
     if paired:
         lax.fori_loop(0, nz, own_column, 0)
         lax.fori_loop(nz, nr - 1, other_column, 0)
-        ax_copy(2 * (chunk_at(0) // 2) + x).wait_recv()
+        for k in range(2):
+            ax_copy(k, 2 * (chunk_at(0) // 2) + x).wait_recv()
     else:
         lax.fori_loop(0, nr - 1, own_column, 0)
     backward(0, True)
@@ -369,10 +390,10 @@
         gm_copy(peer, peer).wait_recv()
         return 0
 
-    lax.fori_loop(1, n, gm_start, 0)
-    lax.fori_loop(1, n, gm_wait, 0)
+    lax.fori_loop(1, n, gm_start, 0, unroll=n <= 8)
+    lax.fori_loop(1, n, gm_wait, 0, unroll=n <= 8)
     gamma_new = lax.fori_loop(
-        0, n, lambda i, acc: acc + gams[i], jnp.zeros((1, 128), jnp.float32)
+        0, n, lambda i, acc: acc + gams[i], jnp.zeros((1, 128), jnp.float32), unroll=n <= 8
     )
     small[0:1, :] = gamma_new
     small[1:2, :] = gamma_new / gamma_row
@@ -387,16 +408,18 @@
     if paired:
         for zz in range(nz):
             x_copy(zz).wait_send()
-            ax_copy(2 * zz + x).wait_send()
+            for k in range(2):
+                ax_copy(k, 2 * zz + x).wait_send()
         for t in range(1, nz):
             z_copy(z, lax.rem(z + t, nz)).wait_send()
+            az_copy(1, me, lax.rem(z + t, nz)).wait_send()
 
     def cv_drain(t, _):
         cv_copy(rank, lax.rem(rank + t, total)).wait_send()
         return 0
 
-    lax.fori_loop(1, n, drain, 0)
-    lax.fori_loop(1, total, cv_drain, 0)
+    lax.fori_loop(1, n, drain, 0, unroll=n <= 8)
+    lax.fori_loop(1, total, cv_drain, 0, unroll=n <= 8)
 
 
 def finish(model, resid, direc, grad, small, model_out, resid_out, direc_out, gamma_out, fresh, sem):
@@ -427,7 +450,7 @@
     ns = n // nr
     cr, cs = rows // nr, sets // ns
     paired = ns == 1 and n % 2 == 0 and n > 2 and cs >= 32
-    fa, ga = (cs * 3 // 4 // 8 * 8, cs // 2 // 8 * 8) if paired else (0, 0)
+    fa, ga = (cs * 5 // 8 // 8 * 8, cs * 3 // 8 // 8 * 8) if paired else (0, 0)
     nz, kept = (n // 2, fa) if paired else (1, 8)
     pieces = 4
     f32 = jnp.float32
@@ -461,7 +484,7 @@
             pltpu.VMEM((n, 1, 128), f32),
             dma((nr,)), dma((6,)),
             dma((nz,)), dma((nz,)), dma((nz,)), dma((nz,)),
-            dma((nz,)), dma((nz,)), dma((nz,)), dma((nz,)),
+            dma((2, nz)), dma((2, nz)), dma((2, nz)), dma((2, nz)),
             dma((n,)), dma((n,)), dma((n,)), dma((n,)),
             dma((2 * n,)), dma((2 * n,)), dma((pieces,)), dma((pieces,)),
             dma((n,)), dma((n,)),

time: 35.8 us -> 34.1 us (0.953)
  Pallas kernels: 35 us -> 33.3 us
    pallas_call x1, Pallas kernels: 33.5 us -> 31.8 us  [local(): pl.pallas_call(functools.partial(kernel, n, nr, ns, fa, ga), out_shape=(p...]
where the time goes in v4:
time: 34.1 us; the launch traced here: 34 us
  Pallas kernels  33.3 us (98%)
  between operations  0.64 us (2%)
    pallas_call x1, Pallas kernels, local(): pl.pallas_call(functools.partial(kernel, n, nr, ns, fa, ga), out_shape=(p...  31.8 us
    pallas_call x1, Pallas kernels, local(): pl.pallas_call(finish, out_shape=(jax.ShapeDtypeStruct(model.shape, f32),...  1.5 us

profile of v4, /device:TPU:0, one launch (start us, length us, event | category | flops | bytes accessed | tf_op | source)
XLA Modules:
  0.0 34.0 jit_solution(18345878026310893646)
XLA Ops:
  0.6 31.8 %cgls_iteration.1 = (f32[64,1024]{1,0:T(8,128)S(1)}, f32[64,2048]{1,0:T(8,128)S(1)}, f32[64,1024]{1,0:T(8,128)S(1)}, f32[4,64,256]{2,1,0:T(8,128)S(1)}, f32[8,128]{1,0:T(8,128)S(1)}) custom-call(bf16[2048,1024]{1,0:T(8,128)(2,1)} %sens_hbm.1, f32[8,16]{1,0:T(8,128)} %bitcast.1, f32[1024]{0:T(1024)} %depth_hbm.1, f32[64,1024]{1,0:T(8,128)} %model_hbm.1, ...), custom_call_target="tpu_custom_call" | custom-call | flops 536870912 | bytes 4194304 | tf_op jit(solution)/shard_map/cgls_iteration/pallas_call | solution.py:460
  32.5 1.5 %cgls_results.1 = (f32[64,1024]{1,0:T(8,128)}, f32[64,2048]{1,0:T(8,128)}, f32[64,1024]{1,0:T(8,128)}, f32[64]{0:T(128)}) custom-call(f32[64,1024]{1,0:T(8,128)S(1)} %get-tuple-element.9.model, f32[64,2048]{1,0:T(8,128)S(1)} %get-tuple-element.10.resid, f32[64,1024]{1,0:T(8,128)S(1)} %get-tuple-element.11.direc, f32[4,64,256]{2,1,0:T(8,128)S(1)} %get-tuple-element.12.grad, ...), custom_call_target="tpu_custom_call" | custom-call | tf_op jit(solution)/shard_map/cgls_results/pallas_call | solution.py:500

commit v5 on v4

--- a/solution.py
+++ b/solution.py
@@ -167,8 +167,8 @@
 
         lax.fori_loop(0, nz, across, 0)
         lax.fori_loop(nz, n - 1, along, 0)
+        lax.fori_loop(0, nz - 1, pass_on, 0, unroll=n <= 8)
         forward(n - 1)
-        lax.fori_loop(0, nz - 1, pass_on, 0, unroll=n <= 8)
     else:
         pl.semaphore_wait(barrier, total - 1)
 
@@ -435,12 +435,11 @@
     for p in range(pieces):
         span = slice(p * width, (p + 1) * width)
         fresh[:, span] = grad[p] + ratio * direc[:, span]
-    last = pltpu.make_async_copy(fresh, direc_out, sem.at[2])
-    last.start()
+        copies.append(pltpu.make_async_copy(fresh.at[:, span], direc_out.at[:, span], sem.at[2 + p]))
+        copies[-1].start()
     gamma_out[...] = small[0, :sets]
     for copy in copies:
         copy.wait()
-    last.wait()
 
 
 def local(n, sensitivity, block_scale, depth_weight, model, residual, direction, gamma):
@@ -507,7 +506,7 @@
         ),
         in_specs=[vmem] * 5,
         out_specs=(hbm, hbm, hbm, vmem),
-        scratch_shapes=[pltpu.VMEM(direction.shape, f32), dma((3,))],
+        scratch_shapes=[pltpu.VMEM(direction.shape, f32), dma((2 + pieces,))],
         compiler_params=pltpu.CompilerParams(vmem_limit_bytes=16 * 1024 * 1024),
         name="cgls_results",
     )(*parts)

time: 34.1 us -> 34.1 us (level)
  no operation moved by 1% of the time
where the time goes in v5:
time: 34.1 us; the launch traced here: 34 us
  Pallas kernels  33.3 us (98%)
  between operations  0.64 us (2%)
    pallas_call x1, Pallas kernels, local(): pl.pallas_call(functools.partial(kernel, n, nr, ns, fa, ga), out_shape=(p...  31.8 us
    pallas_call x1, Pallas kernels, local(): pl.pallas_call(finish, out_shape=(jax.ShapeDtypeStruct(model.shape, f32),...  1.52 us

profile of v5, /device:TPU:0, one launch (start us, length us, event | category | flops | bytes accessed | tf_op | source)
XLA Modules:
  0.0 34.0 jit_solution(1600862309333257551)
XLA Ops:
  0.6 31.8 %cgls_iteration.1 = (f32[64,1024]{1,0:T(8,128)S(1)}, f32[64,2048]{1,0:T(8,128)S(1)}, f32[64,1024]{1,0:T(8,128)S(1)}, f32[4,64,256]{2,1,0:T(8,128)S(1)}, f32[8,128]{1,0:T(8,128)S(1)}) custom-call(bf16[2048,1024]{1,0:T(8,128)(2,1)} %sens_hbm.1, f32[8,16]{1,0:T(8,128)} %bitcast.1, f32[1024]{0:T(1024)} %depth_hbm.1, f32[64,1024]{1,0:T(8,128)} %model_hbm.1, ...), custom_call_target="tpu_custom_call" | custom-call | flops 536870912 | bytes 4194304 | tf_op jit(solution)/shard_map/cgls_iteration/pallas_call | solution.py:459
  32.5 1.5 %cgls_results.1 = (f32[64,1024]{1,0:T(8,128)}, f32[64,2048]{1,0:T(8,128)}, f32[64,1024]{1,0:T(8,128)}, f32[64]{0:T(128)}) custom-call(f32[64,1024]{1,0:T(8,128)S(1)} %get-tuple-element.9.model, f32[64,2048]{1,0:T(8,128)S(1)} %get-tuple-element.10.resid, f32[64,1024]{1,0:T(8,128)S(1)} %get-tuple-element.11.direc, f32[4,64,256]{2,1,0:T(8,128)S(1)} %get-tuple-element.12.grad, ...), custom_call_target="tpu_custom_call" | custom-call | tf_op jit(solution)/shard_map/cgls_results/pallas_call | solution.py:499
